TPU v7x, 32 devices: a whole 2x2x4 slice. The times are simulated.
32 devices in a mesh: worker: 2 (over x), shard: 16 (over z, y, core).
Axes of the slice: x: 2, y: 2, z: 4, core: 2. Of those that a mesh axis runs over, the one named last changes fastest.
Arguments:
- acts: bfloat16 [16384, 8192], P(('worker', 'shard')), may hold values from -6 to 6
- out_grads: bfloat16 [16384, 1024], P(('worker', 'shard')), may hold values from -6 to 6
- local_weight: bfloat16 [2, 1024, 8192], P('worker', 'shard'), may hold values from -6.1 to 6.1
- adam_mean: float32 [2, 1024, 8192], P('worker', 'shard'), may hold values from -0.6 to 0.6
- adam_var: float32 [2, 1024, 8192], P('worker', 'shard'), may hold values from 0.05 to 2
- global_weight: float32 [1024, 8192], P('shard', 'worker'), may hold values from -6 to 6
- outer_momentum: float32 [1024, 8192], P('shard', 'worker'), may hold values from -0.12 to 0.12
- step_count: int32 [1], replicated, may hold values from 1 to 8
Outputs:
- synced_weight: bfloat16 [1024, 8192], P('shard')
- new_global: float32 [1024, 8192], P('shard', 'worker')
- new_momentum: float32 [1024, 8192], P('shard', 'worker')
All inputs are finite; a program needn't handle non-finite values.
Results may differ from a plain program's by a relative error of at most 0.012.
Values may be sent and summed in bfloat16 or wider, within the bound.
A program may use at most 128 MiB of HBM per device.

v0:
```python
import math

import jax
import jax.numpy as jnp
from jax import lax
from jax.sharding import PartitionSpec as P


def inner_step(weight, mean, var, grad, count):
    moment = 0.9 * mean + 0.1 * grad
    second = 0.95 * var + 0.05 * grad * grad
    first_fix = 1.0 - jnp.power(0.9, count)
    second_fix = 1.0 - jnp.power(0.95, count)
    ratio = moment / first_fix / (jnp.sqrt(second / second_fix) + 1e-08)
    return weight - 0.1 * (ratio + 0.1 * weight)


def local(
    acts, out_grads, local_weight, adam_mean, adam_var, global_weight, outer_momentum, step_count
):
    shards = lax.axis_size("shard")
    workers = lax.axis_size("worker")
    units = local_weight.shape[1]
    tokens = acts.shape[0]
    factor = 1.0 / math.sqrt(tokens * shards)
    count = step_count[0].astype(jnp.float32)
    blocks = 1
    share = units // blocks
    arranged = out_grads.reshape(tokens, shards, blocks, share)
    picked = arranged[:, :, 0, :].reshape(tokens, shards * share)

    def gradient_term(start, rows, picked=picked):
        return (
            lax.dot_general(
                picked, acts, (((0,), (0,)), ((), ())), preferred_element_type=jnp.float32
            )
            * factor
        )

    grad = lax.psum_scatter(
        gradient_term(jnp.int32(0), lax.axis_size("shard") * share).astype(jnp.bfloat16),
        "shard",
        scatter_dimension=0,
        tiled=True,
    ).astype(jnp.float32)
    weight = local_weight[0, 0:share].astype(jnp.float32)
    stepped = inner_step(weight, adam_mean[0, 0:share], adam_var[0, 0:share], grad, count)
    summed = lax.psum_scatter(stepped, "worker", scatter_dimension=1, tiled=True)
    delta = global_weight - summed / workers
    momentum = 0.9 * outer_momentum + delta
    updated = global_weight - 0.7 * (delta + 0.9 * momentum)
    synced = lax.all_gather(updated.astype(jnp.bfloat16), "worker", axis=1, tiled=True)
    return (synced, updated, momentum)


def solution(mesh):
    placed = (
        P(("worker", "shard"), None),
        P(("worker", "shard"), None),
        P("worker", "shard", None),
        P("worker", "shard", None),
        P("worker", "shard", None),
        P("shard", "worker"),
        P("shard", "worker"),
        P(),
    )
    return jax.shard_map(
        local,
        mesh=mesh,
        in_specs=placed,
        out_specs=(P("shard", None), P("shard", "worker"), P("shard", "worker")),
        check_vma=False,
    )
```

profile of v0, /device:TPU:0, one launch (start us, length us, event | category | flops | bytes accessed | tf_op | source)
XLA Modules:
  0.0 275.2 jit_solution(2846200837553988054)
XLA Ops:
  7.2 0.0 copy-start
  7.2 0.0 reduce-scatter.3.cloned.1.call-start
  7.2 1.2 copy-done
  8.4 15.8 %multiply_convert_fusion = bf16[1024,8192]{1,0:T(8,128)(2,1)} fusion(bf16[512,1024]{1,0:T(8,128)(2,1)S(1)} %copy-done, bf16[512,8192]{1,0:T(8,128)(2,1)} %param.8), kind=kOutput, calls=%fused_computation | convolution fusion | flops 8606711808 | bytes 26214400 | tf_op jit(solution)/shard_map/dot_general | solution.py:34
  24.2 0.0 copy-start.1
  24.2 0.0 reduce-scatter.3.cloned.1.call-update
  24.3 0.0 reduce-scatter.5.cloned.1.call-start
  25.2 180.5 %reduce-scatter.3.cloned.1.call-done = bf16[64,8192]{1,0:T(8,128)(2,1)} async-done(((bf16[1024,8192]{1,0:T(8,128)(2,1)}), bf16[64,8192]{1,0:T(8,128)(2,1)}) %reduce-scatter.3.cloned.1.call-update) | async-done | bytes 1048592 | tf_op jit(solution)/shard_map/reduce_scatter | solution.py:40
  205.7 0.0 copy-done.1
  205.7 5.2 %convert_subtract_fusion = f32[64,8192]{1,0:T(8,128)} fusion(bf16[64,8192]{1,0:T(8,128)(2,1)} %reduce-scatter.3.cloned.1.call-done, f32[1,64,8192]{2,1,0:T(8,128)S(1)} %copy-done.1, f32[1,64,8192]{2,1,0:T(8,128)} %param.11, bf16[1,64,8192]{2,1,0:T(8,128)(2,1)} %param.10, f32[]{:T(128)} %bitcast.4, f32[]{:T(128)} %bitcast.2), kind=kLoop, calls=%fused_computation.2 | loop fusion | flops 8912896 | bytes 8388616 | tf_op jit(solution)/shard_map/sub | solution.py:15
  210.9 0.0 copy-start.2
  210.9 0.0 copy-start.3
  210.9 0.0 reduce-scatter.5.cloned.1.call-update
  210.9 0.0 all-gather.2.cloned.1.call-start
  211.0 30.9 %reduce-scatter.5.cloned.1.call-done = f32[64,4096]{1,0:T(8,128)} async-done(((f32[64,8192]{1,0:T(8,128)}), f32[64,4096]{1,0:T(8,128)}) %reduce-scatter.5.cloned.1.call-update) | async-done | bytes 1048592 | tf_op jit(solution)/shard_map/reduce_scatter | solution.py:48
  241.9 0.0 copy-done.2
  241.9 0.0 copy-done.3
  241.9 3.0 %fusion.9 = (bf16[64,4096]{1,0:T(8,128)(2,1)}, f32[64,4096]{1,0:T(8,128)}, f32[64,4096]{1,0:T(8,128)}) fusion(f32[64,4096]{1,0:T(8,128)S(1)} %copy-done.2, f32[64,4096]{1,0:T(8,128)} %reduce-scatter.5.cloned.1.call-done, f32[64,4096]{1,0:T(8,128)S(1)} %copy-done.3), kind=kLoop, calls=%fused_computation.17 | loop fusion | flops 2359296 | bytes 5767168 | tf_op jit(solution)/shard_map/convert_element_type | solution.py:52
  244.9 0.0 all-gather.2.cloned.1.call-update
  245.0 21.5 %all-gather.2.cloned.1.call-done = bf16[64,8192]{1,0:T(8,128)(2,1)} async-done(((bf16[64,4096]{1,0:T(8,128)(2,1)}), bf16[64,8192]{1,0:T(8,128)(2,1)}) %all-gather.2.cloned.1.call-update) | async-done | bytes 1048592 | tf_op jit(solution)/shard_map/all_gather | solution.py:52
  266.4 2.3 copy.13
Async XLA Ops:
  7.2 1.2 copy-start
  7.2 198.5 %reduce-scatter.3.cloned.1.call-start = ((), (), s32[]{:S(2)}) async-start(), calls=%async_computation.2 | async-start | bytes 17825792 | tf_op jit(solution)/shard_map/reduce_scatter | solution.py:40
  24.2 181.4 %copy-start.1 = (f32[1,64,8192]{2,1,0:T(8,128)S(1)}, f32[1,64,8192]{2,1,0:T(8,128)}, u32[]{:S(2)}) copy-start(f32[1,64,8192]{2,1,0:T(8,128)} %param.12) | copy-start | bytes 6291460
  24.3 217.6 %reduce-scatter.5.cloned.1.call-start = ((), (), s32[]{:S(2)}) async-start(), calls=%async_computation.3 | async-start | bytes 3145728 | tf_op jit(solution)/shard_map/reduce_scatter | solution.py:48
  210.9 31.0 %copy-start.2 = (f32[64,4096]{1,0:T(8,128)S(1)}, f32[64,4096]{1,0:T(8,128)}, u32[]{:S(2)}) copy-start(f32[64,4096]{1,0:T(8,128)} %param.13) | copy-start | bytes 3145732
  210.9 31.0 %copy-start.3 = (f32[64,4096]{1,0:T(8,128)S(1)}, f32[64,4096]{1,0:T(8,128)}, u32[]{:S(2)}) copy-start(f32[64,4096]{1,0:T(8,128)} %param.14) | copy-start | bytes 3145732
  210.9 55.5 %all-gather.2.cloned.1.call-start = ((), (), s32[]{:S(2)}) async-start(), calls=%async_computation.4 | async-start | bytes 1572864 | tf_op jit(solution)/shard_map/all_gather | solution.py:52
Sparse Core Ops, SparseCore 0:
  24.4 181.2 reduce-scatter.2
  211.0 30.8 reduce-scatter.4
  245.1 21.3 all-gather.1
where the time goes:
time: 276 us; the launch traced here: 275 us
  waiting for transfers between devices  233 us (84%)
  matrix products  15.8 us (6%)
  between operations  14.6 us (5%)
  other arithmetic  8.26 us (3%)
  local copies, waits for them, and re-layouts  3.45 us (1%)
    reduce_scatter x1, waiting for transfers between devices, local(): lax.psum_scatter(gradient_term(jnp.int32(0), lax.axis_size('shard') * sha...  180 us
    reduce_scatter x1, waiting for transfers between devices, local(): lax.psum_scatter(stepped, 'worker', scatter_dimension=1, tiled=True)  30.9 us
    all_gather x1, waiting for transfers between devices, local(): lax.all_gather(updated.astype(jnp.bfloat16), 'worker', axis=1, tiled=True)  21.5 us
    dot_general x1, matrix products, gradient_term(): lax.dot_general(picked, acts, (((0,), (0,)), ((), ())), preferred_element...  15.8 us
  transfers between devices with their start and end apart: 3, of which 3 were waited for; matrix products, arithmetic and copies ran while one was open for 0% of the time, Pallas kernels for 0%

commit v1 on v0

v1 whole, which is shorter than its diff:
```python
import functools
import math

import jax
import jax.numpy as jnp
from jax import lax
from jax.experimental import pallas as pl
from jax.experimental.pallas import tpu as pltpu
from jax.sharding import PartitionSpec as P

CORES = 2
ROWS_Y = 2
LAYERS_Z = 4
CHUNKS = 16
LAG_Y = 3
LAG_Z = 5
LAG_CORE = 6
LAG_RATIO = 7


def inner_step(weight, mean, var, grad, count):
    moment = 0.9 * mean + 0.1 * grad
    second = 0.95 * var + 0.05 * grad * grad
    first_fix = 1.0 - jnp.power(0.9, count)
    second_fix = 1.0 - jnp.power(0.95, count)
    ratio = moment / first_fix / (jnp.sqrt(second / second_fix) + 1e-08)
    return weight - 0.1 * (ratio + 0.1 * weight)


def plain(
    acts, out_grads, local_weight, adam_mean, adam_var, global_weight, outer_momentum, step_count
):
    shards = lax.axis_size("shard")
    workers = lax.axis_size("worker")
    factor = 1.0 / math.sqrt(acts.shape[0] * shards)
    count = step_count[0].astype(jnp.float32)
    term = lax.dot_general(
        out_grads, acts, (((0,), (0,)), ((), ())), preferred_element_type=jnp.float32
    )
    grad = lax.psum_scatter(
        (term * factor).astype(jnp.bfloat16), "shard", scatter_dimension=0, tiled=True
    ).astype(jnp.float32)
    weight = local_weight[0].astype(jnp.float32)
    stepped = inner_step(weight, adam_mean[0], adam_var[0], grad, count)
    summed = lax.psum_scatter(stepped, "worker", scatter_dimension=1, tiled=True)
    delta = global_weight - summed / workers
    momentum = 0.9 * outer_momentum + delta
    updated = global_weight - 0.7 * (delta + 0.9 * momentum)
    synced = lax.all_gather(updated.astype(jnp.bfloat16), "worker", axis=1, tiled=True)
    return (synced, updated, momentum)


def kernel(
    factor, acts, grads, weight, mean, var, glob, outer, count,
    synced, new_glob, new_mom,
    a, g, gt, p, yin, zin, cout, gbuf, rout, rin, acc, ng, nm, sy, wv, mv, vv, gv, ov, wo,
    a_loc, a_out, a_in, gt_out, gt_in, y_out, y_in, z_out, z_in, c_out, c_in, r_out, r_in,
    s_out, s_in, w_out, w_in, loads, stores,
):
    r = lax.axis_index("worker")
    s = lax.axis_index("shard")
    z = lax.div(s, 4)
    y = lax.rem(lax.div(s, 2), 2)
    k = lax.rem(s, 2)
    tokens = acts.shape[0]
    chunks, _, cols = a.shape
    half = chunks * cols
    rows = yin.shape[1]
    units = gbuf.shape[2]
    block = CORES * units
    other_core = (r, z * 4 + y * 2 + 1 - k)
    other_y = (r, z * 4 + (1 - y) * 2 + k)
    other_worker = (1 - r, s)
    zs = [lax.rem(z + d, 4) for d in (1, 2, 3)]
    others_z = [(r, t * 4 + y * 2 + k) for t in zs]

    def remote(src, dst, send, recv, to):
        return pltpu.make_async_remote_copy(
            src_ref=src, dst_ref=dst, send_sem=send, recv_sem=recv,
            device_id=to, device_id_type=pl.DeviceIdType.MESH,
        )

    def at(start, step=cols):
        return pl.ds(pl.multiple_of(start, step), step)

    def acts_local(c):
        return pltpu.make_async_copy(
            acts.at[:, at(k * half + c * cols)], a.at[c, pl.ds(0, tokens)], a_loc.at[c]
        )

    def acts_remote(c):
        return remote(
            acts.at[:, at((1 - k) * half + c * cols)], a.at[c, pl.ds(tokens, tokens)],
            a_out.at[c], a_in.at[c], other_core,
        )

    def y_copy(c):
        return remote(
            p.at[c, at((1 - y) * rows, rows)], yin.at[c], y_out.at[c], y_in.at[c], other_y
        )

    def z_copy(c, d):
        return remote(
            p.at[c, at(y * rows + zs[d] * block, block)], zin.at[c, d],
            z_out.at[c, d], z_in.at[c, d], others_z[d],
        )

    def core_copy(c):
        return remote(cout.at[c], gbuf.at[c, k], c_out.at[c], c_in.at[c], other_core)

    def ratio_copy(c):
        return remote(rout.at[c], rin.at[c], r_out.at[c], r_in.at[c], other_worker)

    def synced_copy(c):
        return remote(
            sy.at[c], synced.at[:, at(r * half + c * cols)], s_out.at[c], s_in.at[c], other_worker
        )

    def stores_of(c):
        return [
            pltpu.make_async_copy(sy.at[c], synced.at[:, at(r * half + c * cols)], stores.at[0, c]),
            pltpu.make_async_copy(ng.at[c], new_glob.at[:, at(c * cols)], stores.at[1, c]),
            pltpu.make_async_copy(nm.at[c], new_mom.at[:, at(c * cols)], stores.at[2, c]),
        ]

    grads_in = pltpu.make_async_copy(grads, g, loads.at[0])
    grads_in.start()

    @pl.loop(0, chunks)
    def _(c):
        acts_local(c).start()

    others = [
        pltpu.make_async_copy(x, v, loads.at[1 + j])
        for j, (x, v) in enumerate(
            ((weight, wv), (mean, mv), (var, vv), (glob, gv), (outer, ov))
        )
    ]
    for copy in others:
        copy.start()

    barrier = pltpu.get_barrier_semaphore()
    for peer in (other_core, other_y, other_worker, *others_z):
        pl.semaphore_signal(barrier, inc=1, device_id=peer, device_id_type=pl.DeviceIdType.MESH)
    pl.semaphore_wait(barrier, 6)

    @pl.loop(0, chunks)
    def _(c):
        acts_remote(c).start()

    weight_copy = remote(
        weight.at[:, at((1 - r) * half, half)], wo, w_out, w_in, other_worker
    )
    weight_copy.start()

    grads_in.wait()
    for j in range(g.shape[1] // block):
        place = (j % ROWS_Y) * LAYERS_Z + j // ROWS_Y
        gt[place * block : (place + 1) * block, 0:tokens] = g[:, j * block : (j + 1) * block].T
    gt_copy = remote(
        gt.at[:, pl.ds(0, tokens)], gt.at[:, pl.ds(tokens, tokens)], gt_out, gt_in, other_core
    )
    gt_copy.start()
    for copy in others:
        copy.wait()
    gt_copy.wait_recv()
    weight_copy.wait_recv()

    time = jnp.full((1, cols), count[0].astype(jnp.float32))
    first = 1.0 / (1.0 - jnp.exp(time * math.log(0.9)))
    second_inv = 1.0 / (1.0 - jnp.exp(time * math.log(0.95)))

    def ratio_of(c, side):
        where = at(side * half + c * cols)
        grad = gbuf[c, side].astype(jnp.float32) * factor
        moment = 0.9 * mv[:, where] + 0.1 * grad
        second = 0.95 * vv[:, where] + 0.05 * grad * grad
        return moment * first / (jnp.sqrt(second * second_inv) + 1e-08)

    def product(c, side):
        p[c, at(side * rows, rows)] = jnp.dot(
            gt[at(side * rows, rows)], a[c], preferred_element_type=jnp.float32
        ).astype(jnp.bfloat16)

    @pl.loop(0, chunks + LAG_RATIO)
    def _(i):
        @pl.when(i < chunks)
        def _():
            c = i
            acts_local(c).wait()
            acts_remote(c).wait_recv()
            product(c, 1 - y)
            y_copy(c).start()
            product(c, y)

        @pl.when((i >= LAG_Y) & (i < chunks + LAG_Y))
        def _():
            c = i - LAG_Y
            y_copy(c).wait_recv()
            mine = at(y * rows, rows)
            p[c, mine] = (
                p[c, mine].astype(jnp.float32) + yin[c].astype(jnp.float32)
            ).astype(jnp.bfloat16)
            for d in (1, 0, 2):
                z_copy(c, d).start()

        @pl.when((i >= LAG_Z) & (i < chunks + LAG_Z))
        def _():
            c = i - LAG_Z
            for d in range(3):
                z_copy(c, d).wait_recv()

            def total(core):
                part = at(core * units, units)
                value = p[c, at(y * rows + z * block + core * units, units)].astype(jnp.float32)
                for d in range(3):
                    value += zin[c, d, part].astype(jnp.float32)
                return value.astype(jnp.bfloat16)

            cout[c] = total(1 - k)
            core_copy(c).start()
            gbuf[c, k] = total(k)

        @pl.when((i >= LAG_CORE) & (i < chunks + LAG_CORE))
        def _():
            c = i - LAG_CORE
            core_copy(c).wait_recv()
            rout[c] = ratio_of(c, 1 - r).astype(jnp.bfloat16)
            ratio_copy(c).start()
            own = wv[:, at(r * half + c * cols)].astype(jnp.float32)
            acc[c] = own - 0.1 * (ratio_of(c, r) + 0.1 * own)

        @pl.when(i >= LAG_RATIO)
        def _():
            c = i - LAG_RATIO
            ratio_copy(c).wait_recv()
            where = at(c * cols)
            its = wo[:, where].astype(jnp.float32)
            summed = acc[c] + (its - 0.1 * (rin[c].astype(jnp.float32) + 0.1 * its))
            delta = gv[:, where] - summed * 0.5
            momentum = 0.9 * ov[:, where] + delta
            updated = gv[:, where] - 0.7 * (delta + 0.9 * momentum)
            sy[c] = updated.astype(jnp.bfloat16)
            synced_copy(c).start()
            ng[c] = updated
            nm[c] = momentum
            for copy in stores_of(c):
                copy.start()

    weight_copy.wait_send()
    gt_copy.wait_send()

    @pl.loop(0, chunks)
    def _(c):
        acts_remote(c).wait_send()
        y_copy(c).wait_send()
        for d in range(3):
            z_copy(c, d).wait_send()
        core_copy(c).wait_send()
        ratio_copy(c).wait_send()
        synced_copy(c).wait()
        for copy in stores_of(c):
            copy.wait()


def fused(
    acts, out_grads, local_weight, adam_mean, adam_var, global_weight, outer_momentum, step_count
):
    tokens, width = acts.shape
    features = out_grads.shape[1]
    units = local_weight.shape[1]
    half = width // CORES
    cols = half // CHUNKS
    rows = features // ROWS_Y
    factor = 1.0 / math.sqrt(tokens * lax.axis_size("shard"))
    b16, f32 = jnp.bfloat16, jnp.float32
    vmem, dma = pltpu.VMEM, pltpu.SemaphoreType.DMA
    n = CHUNKS
    return pl.pallas_call(
        functools.partial(kernel, factor),
        out_shape=(
            jax.ShapeDtypeStruct((units, width), b16),
            jax.ShapeDtypeStruct((units, half), f32),
            jax.ShapeDtypeStruct((units, half), f32),
        ),
        in_specs=[pl.BlockSpec(memory_space=pl.ANY)] * 7
        + [pl.BlockSpec(memory_space=pltpu.SMEM)],
        out_specs=[pl.BlockSpec(memory_space=pl.ANY)] * 3,
        scratch_shapes=[
            vmem((n, CORES * tokens, cols), b16),
            vmem((tokens, features), b16),
            vmem((features, CORES * tokens), b16),
            vmem((n, features, cols), b16),
            vmem((n, rows, cols), b16),
            vmem((n, LAYERS_Z - 1, CORES * units, cols), b16),
            vmem((n, units, cols), b16),
            vmem((n, CORES, units, cols), b16),
            vmem((n, units, cols), b16),
            vmem((n, units, cols), b16),
            vmem((n, units, cols), f32),
            vmem((n, units, cols), f32),
            vmem((n, units, cols), f32),
            vmem((n, units, cols), b16),
            vmem((units, width), b16),
            vmem((units, width), f32),
            vmem((units, width), f32),
            vmem((units, half), f32),
            vmem((units, half), f32),
            vmem((units, half), b16),
            dma((n,)), dma((n,)), dma((n,)), dma, dma,
            dma((n,)), dma((n,)), dma((n, 3)), dma((n, 3)),
            dma((n,)), dma((n,)), dma((n,)), dma((n,)),
            dma((n,)), dma((n,)), dma, dma, dma((6,)), dma((3, n)),
        ],
        compiler_params=pltpu.CompilerParams(
            collective_id=0, has_side_effects=True, vmem_limit_bytes=56 * 2**20
        ),
        cost_estimate=pl.CostEstimate(
            flops=2 * tokens * width * features, bytes_accessed=24 * 2**20, transcendentals=0
        ),
    )(
        acts, out_grads, local_weight[0], adam_mean[0], adam_var[0],
        global_weight, outer_momentum, step_count,
    )


def solution(mesh):
    placed = (
        P(("worker", "shard"), None),
        P(("worker", "shard"), None),
        P("worker", "shard", None),
        P("worker", "shard", None),
        P("worker", "shard", None),
        P("shard", "worker"),
        P("shard", "worker"),
        P(),
    )
    grid = (2, CORES * ROWS_Y * LAYERS_Z)
    return jax.shard_map(
        fused if (mesh.shape["worker"], mesh.shape["shard"]) == grid else plain,
        mesh=mesh,
        in_specs=placed,
        out_specs=(P("shard", None), P("shard", "worker"), P("shard", "worker")),
        check_vma=False,
    )
```

time: 276 us -> 133 us (0.48)
  waiting for transfers between devices: 233 us -> 0 us
  Pallas kernels: 0 us -> 127 us
  matrix products: 15.8 us -> 0 us
  between operations: 14.6 us -> 1.31 us
  other arithmetic: 8.26 us -> 0 us
    reduce_scatter x2 -> x0, waiting for transfers between devices: 211 us -> none  [the longest x1 180 us: local(): lax.psum_scatter(gradient_term(jnp.int32(0), lax.axis_size('shard') * sha...]
    pallas_call x0 -> x1, Pallas kernels: none -> 127 us  [fused(): pl.pallas_call(functools.partial(kernel, factor), out_shape=(jax.ShapeDty...]
    all_gather x1 -> x0, waiting for transfers between devices: 21.5 us -> none  [local(): lax.all_gather(updated.astype(jnp.bfloat16), 'worker', axis=1, tiled=True)]
    dot_general x1 -> x0, matrix products: 15.8 us -> none  [gradient_term(): lax.dot_general(picked, acts, (((0,), (0,)), ((), ())), preferred_element...]
    sub x1 -> x0, other arithmetic: 5.21 us -> none  [inner_step(): return weight - 0.1 * (ratio + 0.1 * weight)]
    convert_element_type x1 -> x0, other arithmetic: 3.04 us -> none  [local(): updated.astype(jnp.bfloat16)]
  transfers between devices with their start and end apart: 3 -> 0, of which waited for: 3 -> 0; matrix products, arithmetic and copies ran while one was open for 0% -> 0% of each run, Pallas kernels for 0% -> 0%
where the time goes in v1:
time: 133 us
  Pallas kernels  127 us (95%)
  local copies, waits for them, and re-layouts  4.36 us (3%)
    pallas_call x1, Pallas kernels, fused(): pl.pallas_call(functools.partial(kernel, factor), out_shape=(jax.ShapeDty...  127 us
    unnamed x7, local copies, waits for them, and re-layouts  4.36 us

profile of v1, /device:TPU:0, one launch (start us, length us, event | category | flops | bytes accessed | tf_op | source)
XLA Modules:
  0.0 132.6 jit_solution(6660189512966243317)
XLA Ops:
  1.3 127.0 %shard_map.103 = (bf16[64,8192]{1,0:T(8,128)(2,1)}, f32[64,4096]{1,0:T(8,128)}, f32[64,4096]{1,0:T(8,128)}) custom-call(bf16[512,8192]{1,0:T(8,128)(2,1)} %acts.1, bf16[512,1024]{1,0:T(8,128)(2,1)} %grads.1, bf16[64,8192]{1,0:T(8,128)(2,1)} %bitcast.5, f32[64,8192]{1,0:T(8,128)} %bitcast.3, f32[64,8192]{1,0:T(8,128)} %bitcast.4, f32[64,4096]{1,0:T(8,128)} %glob.1, ...), custom_call_target="tpu_custom_call" | custom-call | flops 8589934592 | bytes 25165824 | tf_op jit(solution)/shard_map/pallas_call | solution.py:279
  128.3 0.0 copy-start.1
  128.3 0.0 copy-start
  128.3 2.4 %copy.15 = bf16[64,8192]{1,0:T(8,128)(2,1)} copy(bf16[64,8192]{1,0:T(8,128)(2,1)} %get-tuple-element.6) | data formatting | bytes 2097152
  130.7 0.0 copy-done.1
  130.7 1.0 copy.16
  131.7 0.0 copy-done
  131.7 1.0 copy.17
Async XLA Ops:
  128.3 2.4 %copy-start.1 = (f32[64,4096]{1,0:T(8,128)S(1)}, f32[64,4096]{1,0:T(8,128)}, u32[]{:S(2)}) copy-start(f32[64,4096]{1,0:T(8,128)} %get-tuple-element.7) | copy-start | bytes 3145732
  128.3 3.4 %copy-start = (f32[64,4096]{1,0:T(8,128)S(1)}, f32[64,4096]{1,0:T(8,128)}, u32[]{:S(2)}) copy-start(f32[64,4096]{1,0:T(8,128)} %get-tuple-element.8) | copy-start | bytes 3145732

commit v2 on v1

--- a/solution.py
+++ b/solution.py
@@ -16,6 +16,7 @@
 LAG_Z = 5
 LAG_CORE = 6
 LAG_RATIO = 7
+LAG_DONE = 8
 
 
 def inner_step(weight, mean, var, grad, count):
@@ -142,16 +143,6 @@
     barrier = pltpu.get_barrier_semaphore()
     for peer in (other_core, other_y, other_worker, *others_z):
         pl.semaphore_signal(barrier, inc=1, device_id=peer, device_id_type=pl.DeviceIdType.MESH)
-    pl.semaphore_wait(barrier, 6)
-
-    @pl.loop(0, chunks)
-    def _(c):
-        acts_remote(c).start()
-
-    weight_copy = remote(
-        weight.at[:, at((1 - r) * half, half)], wo, w_out, w_in, other_worker
-    )
-    weight_copy.start()
 
     grads_in.wait()
     for j in range(g.shape[1] // block):
@@ -160,11 +151,18 @@
     gt_copy = remote(
         gt.at[:, pl.ds(0, tokens)], gt.at[:, pl.ds(tokens, tokens)], gt_out, gt_in, other_core
     )
+    weight_copy = remote(
+        weight.at[:, at((1 - r) * half, half)], wo, w_out, w_in, other_worker
+    )
+    pl.semaphore_wait(barrier, 6)
     gt_copy.start()
-    for copy in others:
-        copy.wait()
+
+    @pl.loop(0, chunks)
+    def _(c):
+        acts_remote(c).start()
+
+    weight_copy.start()
     gt_copy.wait_recv()
-    weight_copy.wait_recv()
 
     time = jnp.full((1, cols), count[0].astype(jnp.float32))
     first = 1.0 / (1.0 - jnp.exp(time * math.log(0.9)))
@@ -182,7 +180,7 @@
             gt[at(side * rows, rows)], a[c], preferred_element_type=jnp.float32
         ).astype(jnp.bfloat16)
 
-    @pl.loop(0, chunks + LAG_RATIO)
+    @pl.loop(0, chunks + LAG_DONE)
     def _(i):
         @pl.when(i < chunks)
         def _():
@@ -221,6 +219,12 @@
             core_copy(c).start()
             gbuf[c, k] = total(k)
 
+        @pl.when(i == LAG_CORE)
+        def _():
+            for copy in others:
+                copy.wait()
+            weight_copy.wait()
+
         @pl.when((i >= LAG_CORE) & (i < chunks + LAG_CORE))
         def _():
             c = i - LAG_CORE
@@ -230,7 +234,7 @@
             own = wv[:, at(r * half + c * cols)].astype(jnp.float32)
             acc[c] = own - 0.1 * (ratio_of(c, r) + 0.1 * own)
 
-        @pl.when(i >= LAG_RATIO)
+        @pl.when((i >= LAG_RATIO) & (i < chunks + LAG_RATIO))
         def _():
             c = i - LAG_RATIO
             ratio_copy(c).wait_recv()
@@ -247,20 +251,20 @@
             for copy in stores_of(c):
                 copy.start()
 
-    weight_copy.wait_send()
+        @pl.when(i >= LAG_DONE)
+        def _():
+            c = i - LAG_DONE
+            acts_remote(c).wait_send()
+            y_copy(c).wait_send()
+            for d in range(3):
+                z_copy(c, d).wait_send()
+            core_copy(c).wait_send()
+            ratio_copy(c).wait_send()
+            synced_copy(c).wait()
+            for copy in stores_of(c):
+                copy.wait()
+
     gt_copy.wait_send()
-
-    @pl.loop(0, chunks)
-    def _(c):
-        acts_remote(c).wait_send()
-        y_copy(c).wait_send()
-        for d in range(3):
-            z_copy(c, d).wait_send()
-        core_copy(c).wait_send()
-        ratio_copy(c).wait_send()
-        synced_copy(c).wait()
-        for copy in stores_of(c):
-            copy.wait()
 
 
 def fused(

time: 133 us -> 124 us (0.932)
  Pallas kernels: 127 us -> 118 us
    pallas_call x1, Pallas kernels: 127 us -> 118 us  [fused(): pl.pallas_call(functools.partial(kernel, factor), out_shape=(jax.ShapeDty...]
where the time goes in v2:
time: 124 us
  Pallas kernels  118 us (95%)
  local copies, waits for them, and re-layouts  4.36 us (4%)
  between operations  1.31 us (1%)
    pallas_call x1, Pallas kernels, fused(): pl.pallas_call(functools.partial(kernel, factor), out_shape=(jax.ShapeDty...  118 us
    unnamed x7, local copies, waits for them, and re-layouts  4.36 us

profile of v2, /device:TPU:0, one launch (start us, length us, event | category | flops | bytes accessed | tf_op | source)
XLA Modules:
  0.0 123.9 jit_solution(3798021301781487349)
XLA Ops:
  1.3 118.3 %shard_map.103 = (bf16[64,8192]{1,0:T(8,128)(2,1)}, f32[64,4096]{1,0:T(8,128)}, f32[64,4096]{1,0:T(8,128)}) custom-call(bf16[512,8192]{1,0:T(8,128)(2,1)} %acts.1, bf16[512,1024]{1,0:T(8,128)(2,1)} %grads.1, bf16[64,8192]{1,0:T(8,128)(2,1)} %bitcast.5, f32[64,8192]{1,0:T(8,128)} %bitcast.3, f32[64,8192]{1,0:T(8,128)} %bitcast.4, f32[64,4096]{1,0:T(8,128)} %glob.1, ...), custom_call_target="tpu_custom_call" | custom-call | flops 8589934592 | bytes 25165824 | tf_op jit(solution)/shard_map/pallas_call | solution.py:283
  119.6 0.0 copy-start.1
  119.6 0.0 copy-start
  119.6 2.4 %copy.15 = bf16[64,8192]{1,0:T(8,128)(2,1)} copy(bf16[64,8192]{1,0:T(8,128)(2,1)} %get-tuple-element.6) | data formatting | bytes 2097152
  122.0 0.0 copy-done.1
  122.0 1.0 copy.16
  123.0 0.0 copy-done
  123.0 1.0 copy.17
Async XLA Ops:
  119.6 2.4 %copy-start.1 = (f32[64,4096]{1,0:T(8,128)S(1)}, f32[64,4096]{1,0:T(8,128)}, u32[]{:S(2)}) copy-start(f32[64,4096]{1,0:T(8,128)} %get-tuple-element.7) | copy-start | bytes 3145732
  119.6 3.4 %copy-start = (f32[64,4096]{1,0:T(8,128)S(1)}, f32[64,4096]{1,0:T(8,128)}, u32[]{:S(2)}) copy-start(f32[64,4096]{1,0:T(8,128)} %get-tuple-element.8) | copy-start | bytes 3145732

commit v3 on v2

--- a/solution.py
+++ b/solution.py
@@ -12,11 +12,10 @@
 ROWS_Y = 2
 LAYERS_Z = 4
 CHUNKS = 16
-LAG_Y = 3
-LAG_Z = 5
-LAG_CORE = 6
-LAG_RATIO = 7
-LAG_DONE = 8
+ZFIRST = 2
+LAG_Y = 4
+LAG_Z = 6
+LAG_DONE = 11
 
 
 def inner_step(weight, mean, var, grad, count):
@@ -54,8 +53,8 @@
 def kernel(
     factor, acts, grads, weight, mean, var, glob, outer, count,
     synced, new_glob, new_mom,
-    a, g, gt, p, yin, zin, cout, gbuf, rout, rin, acc, ng, nm, sy, wv, mv, vv, gv, ov, wo,
-    a_loc, a_out, a_in, gt_out, gt_in, y_out, y_in, z_out, z_in, c_out, c_in, r_out, r_in,
+    a, g, gt, p, yin, ybin, lin, rin_z, gbuf, rout, rin, acc, ng, nm, sy, wv, mv, vv, gv, ov, wo,
+    a_loc, a_out, a_in, gt_out, gt_in, y_out, y_in, rz_out, rz_in, lz_out, lz_in, c_out, c_in, r_out, r_in,
     s_out, s_in, w_out, w_in, loads, stores,
 ):
     r = lax.axis_index("worker")
@@ -72,8 +71,8 @@
     other_core = (r, z * 4 + y * 2 + 1 - k)
     other_y = (r, z * 4 + (1 - y) * 2 + k)
     other_worker = (1 - r, s)
-    zs = [lax.rem(z + d, 4) for d in (1, 2, 3)]
-    others_z = [(r, t * 4 + y * 2 + k) for t in zs]
+    firsts = chunks - yin.shape[0]
+    plains = chunks - firsts
 
     def remote(src, dst, send, recv, to):
         return pltpu.make_async_remote_copy(
@@ -100,14 +99,111 @@
             p.at[c, at((1 - y) * rows, rows)], yin.at[c], y_out.at[c], y_in.at[c], other_y
         )
 
-    def z_copy(c, d):
-        return remote(
-            p.at[c, at(y * rows + zs[d] * block, block)], zin.at[c, d],
-            z_out.at[c, d], z_in.at[c, d], others_z[d],
-        )
+    def late_y_copy(c):
+        return remote(
+            p.at[c, at((1 - y) * rows + z * block, block)], ybin.at[c - plains],
+            y_out.at[c], y_in.at[c], other_y,
+        )
+
+    def right_copy(task, c, part, here):
+        size = (LAYERS_Z - 1 - here) * block
+        return remote(
+            p.at[c, pl.ds(pl.multiple_of(part * rows + (here + 1) * block, block), size)],
+            rin_z.at[task, pl.ds(here * block, size)], rz_out.at[task], rz_in.at[task],
+            (r, (here + 1) * 4 + y * 2 + k),
+        )
+
+    def left_copy(task, c, part, here):
+        size = here * block
+        return remote(
+            p.at[c, pl.ds(pl.multiple_of(part * rows, block), size)],
+            lin.at[task, pl.ds(0, size)], lz_out.at[task], lz_in.at[task],
+            (r, (here - 1) * 4 + y * 2 + k),
+        )
+
+    def add_to(c, part, low, high, *arrived):
+        where = pl.ds(pl.multiple_of(part * rows + low * block, block), (high - low) * block)
+        value = p[c, where].astype(jnp.float32)
+        for ref in arrived:
+            value += ref.astype(jnp.float32)
+        p[c, where] = value.astype(jnp.bfloat16)
+
+    def from_left(task, low, high):
+        return rin_z[task, pl.ds((low - 1) * block, (high - low) * block)]
+
+    def from_right(task, low, high):
+        return lin[task, pl.ds(low * block, (high - low) * block)]
+
+    def line_start(task, c, part):
+        @pl.when(z == 0)
+        def _():
+            right_copy(task, c, part, 0).start()
+
+        @pl.when(z == 3)
+        def _():
+            left_copy(task, c, part, 3).start()
+
+    def line_inward(task, c, part):
+        @pl.when(z == 1)
+        def _():
+            right_copy(task, c, part, 0).wait_recv()
+            add_to(c, part, 2, 4, from_left(task, 2, 4))
+            right_copy(task, c, part, 1).start()
+
+        @pl.when(z == 2)
+        def _():
+            left_copy(task, c, part, 3).wait_recv()
+            add_to(c, part, 0, 2, from_right(task, 0, 2))
+            left_copy(task, c, part, 2).start()
+
+    def line_outward(task, c, part):
+        @pl.when(z == 1)
+        def _():
+            left_copy(task, c, part, 2).wait_recv()
+            add_to(c, part, 0, 1, from_right(task, 0, 1))
+            left_copy(task, c, part, 1).start()
+
+        @pl.when(z == 2)
+        def _():
+            right_copy(task, c, part, 1).wait_recv()
+            add_to(c, part, 3, 4, from_left(task, 3, 4))
+            right_copy(task, c, part, 2).start()
+
+    def line_end(task, c, part):
+        @pl.when(z == 0)
+        def _():
+            left_copy(task, c, part, 1).wait_recv()
+            add_to(c, part, 0, 1, from_right(task, 0, 1))
+
+        @pl.when(z == 3)
+        def _():
+            right_copy(task, c, part, 2).wait_recv()
+            add_to(c, part, 3, 4, from_left(task, 3, 4))
+
+        for here in (1, 2):
+
+            @pl.when(z == here)
+            def _(here=here):
+                add_to(
+                    c, part, here, here + 1,
+                    from_left(task, here, here + 1), from_right(task, here, here + 1),
+                )
+
+    def line_sent(task, c, part):
+        for here in range(LAYERS_Z):
+
+            @pl.when(z == here)
+            def _(here=here):
+                if here < LAYERS_Z - 1:
+                    right_copy(task, c, part, here).wait_send()
+                if here > 0:
+                    left_copy(task, c, part, here).wait_send()
 
     def core_copy(c):
-        return remote(cout.at[c], gbuf.at[c, k], c_out.at[c], c_in.at[c], other_core)
+        return remote(
+            p.at[c, at(y * rows + z * block + (1 - k) * units, units)], gbuf.at[c, k],
+            c_out.at[c], c_in.at[c], other_core,
+        )
 
     def ratio_copy(c):
         return remote(rout.at[c], rin.at[c], r_out.at[c], r_in.at[c], other_worker)
@@ -141,8 +237,20 @@
         copy.start()
 
     barrier = pltpu.get_barrier_semaphore()
-    for peer in (other_core, other_y, other_worker, *others_z):
+    for peer in (other_core, other_y, other_worker):
         pl.semaphore_signal(barrier, inc=1, device_id=peer, device_id_type=pl.DeviceIdType.MESH)
+
+    @pl.when(z > 0)
+    def _():
+        pl.semaphore_signal(
+            barrier, inc=1, device_id=(r, s - 4), device_id_type=pl.DeviceIdType.MESH
+        )
+
+    @pl.when(z < 3)
+    def _():
+        pl.semaphore_signal(
+            barrier, inc=1, device_id=(r, s + 4), device_id_type=pl.DeviceIdType.MESH
+        )
 
     grads_in.wait()
     for j in range(g.shape[1] // block):
@@ -154,10 +262,17 @@
     weight_copy = remote(
         weight.at[:, at((1 - r) * half, half)], wo, w_out, w_in, other_worker
     )
-    pl.semaphore_wait(barrier, 6)
+    pl.semaphore_wait(barrier, 4 + lax.rem(lax.div(z + 1, 2), 2))
     gt_copy.start()
 
-    @pl.loop(0, chunks)
+    acts_remote(0).start()
+
+    @pl.loop(0, firsts)
+    def _(j):
+        acts_remote(plains + j).start()
+        acts_remote(1 + j).start()
+
+    @pl.loop(1 + firsts, plains)
     def _(c):
         acts_remote(c).start()
 
@@ -180,89 +295,149 @@
             gt[at(side * rows, rows)], a[c], preferred_element_type=jnp.float32
         ).astype(jnp.bfloat16)
 
-    @pl.loop(0, chunks + LAG_DONE)
+    def fetched(c):
+        acts_local(c).wait()
+        acts_remote(c).wait_recv()
+
+    def to_core(c):
+        core_copy(c).start()
+        gbuf[c, k] = p[c, at(y * rows + z * block + k * units, units)]
+
+    def adam(c):
+        core_copy(c).wait_recv()
+        rout[c] = ratio_of(c, 1 - r).astype(jnp.bfloat16)
+        ratio_copy(c).start()
+        own = wv[:, at(r * half + c * cols)].astype(jnp.float32)
+        acc[c] = own - 0.1 * (ratio_of(c, r) + 0.1 * own)
+
+    def update(c):
+        ratio_copy(c).wait_recv()
+        where = at(c * cols)
+        its = wo[:, where].astype(jnp.float32)
+        summed = acc[c] + (its - 0.1 * (rin[c].astype(jnp.float32) + 0.1 * its))
+        delta = gv[:, where] - summed * 0.5
+        momentum = 0.9 * ov[:, where] + delta
+        updated = gv[:, where] - 0.7 * (delta + 0.9 * momentum)
+        sy[c] = updated.astype(jnp.bfloat16)
+        synced_copy(c).start()
+        ng[c] = updated
+        nm[c] = momentum
+        for copy in stores_of(c):
+            copy.start()
+
+    def done(c):
+        acts_remote(c).wait_send()
+        core_copy(c).wait_send()
+        ratio_copy(c).wait_send()
+        synced_copy(c).wait()
+        for copy in stores_of(c):
+            copy.wait()
+
+    @pl.loop(0, plains + LAG_DONE)
     def _(i):
-        @pl.when(i < chunks)
-        def _():
-            c = i
-            acts_local(c).wait()
-            acts_remote(c).wait_recv()
+        def plain_at(lag):
+            def run(stage):
+                pl.when((i >= lag) & (i < plains + lag))(lambda: stage(i - lag))
+            return run
+
+        def first_at(lag):
+            def run(stage):
+                pl.when((i >= lag) & (i < firsts + lag))(lambda: stage(i - lag + plains))
+            return run
+
+        def halves(stage, c):
+            for h in range(ROWS_Y):
+                task = plains + (c - plains) * ROWS_Y + h
+                stage(task, c, y if h == 1 else 1 - y)
+
+        @plain_at(0)
+        def _(c):
+            fetched(c)
             product(c, 1 - y)
             y_copy(c).start()
             product(c, y)
 
-        @pl.when((i >= LAG_Y) & (i < chunks + LAG_Y))
-        def _():
-            c = i - LAG_Y
+        @first_at(1)
+        def _(c):
+            fetched(c)
+            product(c, 1 - y)
+            product(c, y)
+            halves(line_start, c)
+
+        @plain_at(LAG_Y)
+        def _(c):
             y_copy(c).wait_recv()
-            mine = at(y * rows, rows)
-            p[c, mine] = (
-                p[c, mine].astype(jnp.float32) + yin[c].astype(jnp.float32)
-            ).astype(jnp.bfloat16)
-            for d in (1, 0, 2):
-                z_copy(c, d).start()
-
-        @pl.when((i >= LAG_Z) & (i < chunks + LAG_Z))
-        def _():
-            c = i - LAG_Z
-            for d in range(3):
-                z_copy(c, d).wait_recv()
-
-            def total(core):
-                part = at(core * units, units)
-                value = p[c, at(y * rows + z * block + core * units, units)].astype(jnp.float32)
-                for d in range(3):
-                    value += zin[c, d, part].astype(jnp.float32)
-                return value.astype(jnp.bfloat16)
-
-            cout[c] = total(1 - k)
-            core_copy(c).start()
-            gbuf[c, k] = total(k)
-
-        @pl.when(i == LAG_CORE)
+            add_to(c, y, 0, LAYERS_Z, yin[c])
+            line_start(c, c, y)
+
+        @first_at(4)
+        def _(c):
+            halves(line_inward, c)
+
+        @plain_at(LAG_Z)
+        def _(c):
+            line_inward(c, c, y)
+
+        @first_at(6)
+        def _(c):
+            halves(line_outward, c)
+
+        @plain_at(LAG_Z + 1)
+        def _(c):
+            line_outward(c, c, y)
+
+        @first_at(8)
+        def _(c):
+            halves(line_end, c)
+            late_y_copy(c).start()
+
+        @plain_at(LAG_Z + 2)
+        def _(c):
+            line_end(c, c, y)
+            to_core(c)
+
+        @pl.when(i == LAG_Z + 3)
         def _():
             for copy in others:
                 copy.wait()
             weight_copy.wait()
 
-        @pl.when((i >= LAG_CORE) & (i < chunks + LAG_CORE))
-        def _():
-            c = i - LAG_CORE
-            core_copy(c).wait_recv()
-            rout[c] = ratio_of(c, 1 - r).astype(jnp.bfloat16)
-            ratio_copy(c).start()
-            own = wv[:, at(r * half + c * cols)].astype(jnp.float32)
-            acc[c] = own - 0.1 * (ratio_of(c, r) + 0.1 * own)
-
-        @pl.when((i >= LAG_RATIO) & (i < chunks + LAG_RATIO))
-        def _():
-            c = i - LAG_RATIO
-            ratio_copy(c).wait_recv()
-            where = at(c * cols)
-            its = wo[:, where].astype(jnp.float32)
-            summed = acc[c] + (its - 0.1 * (rin[c].astype(jnp.float32) + 0.1 * its))
-            delta = gv[:, where] - summed * 0.5
-            momentum = 0.9 * ov[:, where] + delta
-            updated = gv[:, where] - 0.7 * (delta + 0.9 * momentum)
-            sy[c] = updated.astype(jnp.bfloat16)
-            synced_copy(c).start()
-            ng[c] = updated
-            nm[c] = momentum
-            for copy in stores_of(c):
-                copy.start()
-
-        @pl.when(i >= LAG_DONE)
-        def _():
-            c = i - LAG_DONE
-            acts_remote(c).wait_send()
+        @plain_at(LAG_Z + 3)
+        def _(c):
+            adam(c)
+
+        @plain_at(LAG_Z + 4)
+        def _(c):
+            update(c)
+
+        @plain_at(LAG_DONE)
+        def _(c):
             y_copy(c).wait_send()
-            for d in range(3):
-                z_copy(c, d).wait_send()
-            core_copy(c).wait_send()
-            ratio_copy(c).wait_send()
-            synced_copy(c).wait()
-            for copy in stores_of(c):
-                copy.wait()
+            line_sent(c, c, y)
+            done(c)
+
+        @first_at(12)
+        def _(c):
+            late_y_copy(c).wait_recv()
+            where = at(y * rows + z * block, block)
+            p[c, where] = (
+                p[c, where].astype(jnp.float32) + ybin[c - plains].astype(jnp.float32)
+            ).astype(jnp.bfloat16)
+            to_core(c)
+
+        @first_at(13)
+        def _(c):
+            adam(c)
+
+        @first_at(14)
+        def _(c):
+            update(c)
+
+        @first_at(15)
+        def _(c):
+            late_y_copy(c).wait_send()
+            halves(line_sent, c)
+            done(c)
 
     gt_copy.wait_send()
 
@@ -280,6 +455,7 @@
     b16, f32 = jnp.bfloat16, jnp.float32
     vmem, dma = pltpu.VMEM, pltpu.SemaphoreType.DMA
     n = CHUNKS
+    tasks = n + ZFIRST * (ROWS_Y - 1)
     return pl.pallas_call(
         functools.partial(kernel, factor),
         out_shape=(
@@ -295,9 +471,10 @@
             vmem((tokens, features), b16),
             vmem((features, CORES * tokens), b16),
             vmem((n, features, cols), b16),
-            vmem((n, rows, cols), b16),
-            vmem((n, LAYERS_Z - 1, CORES * units, cols), b16),
-            vmem((n, units, cols), b16),
+            vmem((n - ZFIRST, rows, cols), b16),
+            vmem((ZFIRST, CORES * units, cols), b16),
+            vmem((tasks, (LAYERS_Z - 1) * CORES * units, cols), b16),
+            vmem((tasks, (LAYERS_Z - 1) * CORES * units, cols), b16),
             vmem((n, CORES, units, cols), b16),
             vmem((n, units, cols), b16),
             vmem((n, units, cols), b16),
@@ -312,7 +489,7 @@
             vmem((units, half), f32),
             vmem((units, half), b16),
             dma((n,)), dma((n,)), dma((n,)), dma, dma,
-            dma((n,)), dma((n,)), dma((n, 3)), dma((n, 3)),
+            dma((n,)), dma((n,)), *[dma((tasks,))] * 4,
             dma((n,)), dma((n,)), dma((n,)), dma((n,)),
             dma((n,)), dma((n,)), dma, dma, dma((6,)), dma((3, n)),
         ],

time: 124 us -> 123 us (level)
  no operation moved by 1% of the time
where the time goes in v3:
time: 123 us
  Pallas kernels  117 us (95%)
  local copies, waits for them, and re-layouts  4.36 us (4%)
  between operations  1.31 us (1%)
    pallas_call x1, Pallas kernels, fused(): pl.pallas_call(functools.partial(kernel, factor), out_shape=(jax.ShapeDty...  117 us
    unnamed x7, local copies, waits for them, and re-layouts  4.36 us

profile of v3, /device:TPU:0, one launch (start us, length us, event | category | flops | bytes accessed | tf_op | source)
XLA Modules:
  0.0 122.8 jit_solution(9836487510989590766)
XLA Ops:
  1.3 117.1 %shard_map.103 = (bf16[64,8192]{1,0:T(8,128)(2,1)}, f32[64,4096]{1,0:T(8,128)}, f32[64,4096]{1,0:T(8,128)}) custom-call(bf16[512,8192]{1,0:T(8,128)(2,1)} %acts.1, bf16[512,1024]{1,0:T(8,128)(2,1)} %grads.1, bf16[64,8192]{1,0:T(8,128)(2,1)} %bitcast.5, f32[64,8192]{1,0:T(8,128)} %bitcast.3, f32[64,8192]{1,0:T(8,128)} %bitcast.4, f32[64,4096]{1,0:T(8,128)} %glob.1, ...), custom_call_target="tpu_custom_call" | custom-call | flops 8589934592 | bytes 25165824 | tf_op jit(solution)/shard_map/pallas_call | solution.py:459
  118.4 0.0 copy-start.1
  118.4 0.0 copy-start
  118.5 2.4 %copy.15 = bf16[64,8192]{1,0:T(8,128)(2,1)} copy(bf16[64,8192]{1,0:T(8,128)(2,1)} %get-tuple-element.6) | data formatting | bytes 2097152
  120.9 0.0 copy-done.1
  120.9 1.0 copy.16
  121.8 0.0 copy-done
  121.8 1.0 copy.17
Async XLA Ops:
  118.4 2.4 %copy-start.1 = (f32[64,4096]{1,0:T(8,128)S(1)}, f32[64,4096]{1,0:T(8,128)}, u32[]{:S(2)}) copy-start(f32[64,4096]{1,0:T(8,128)} %get-tuple-element.7) | copy-start | bytes 3145732
  118.4 3.4 %copy-start = (f32[64,4096]{1,0:T(8,128)S(1)}, f32[64,4096]{1,0:T(8,128)}, u32[]{:S(2)}) copy-start(f32[64,4096]{1,0:T(8,128)} %get-tuple-element.8) | copy-start | bytes 3145732

commit v4 on v3

--- a/solution.py
+++ b/solution.py
@@ -12,10 +12,11 @@
 ROWS_Y = 2
 LAYERS_Z = 4
 CHUNKS = 16
-ZFIRST = 2
-LAG_Y = 4
-LAG_Z = 6
-LAG_DONE = 11
+ZFIRST = 3
+AHEAD = 3
+LAG_Y = 2
+LAG_Z = 5
+LAG_DONE = 10
 
 
 def inner_step(weight, mean, var, grad, count):
@@ -105,20 +106,16 @@
             y_out.at[c], y_in.at[c], other_y,
         )
 
-    def right_copy(task, c, part, here):
-        size = (LAYERS_Z - 1 - here) * block
-        return remote(
-            p.at[c, pl.ds(pl.multiple_of(part * rows + (here + 1) * block, block), size)],
-            rin_z.at[task, pl.ds(here * block, size)], rz_out.at[task], rz_in.at[task],
-            (r, (here + 1) * 4 + y * 2 + k),
-        )
-
-    def left_copy(task, c, part, here):
-        size = here * block
-        return remote(
-            p.at[c, pl.ds(pl.multiple_of(part * rows, block), size)],
-            lin.at[task, pl.ds(0, size)], lz_out.at[task], lz_in.at[task],
-            (r, (here - 1) * 4 + y * 2 + k),
+    def right_copy(task, c, part, here, t):
+        return remote(
+            p.at[c, at(part * rows + t * block, block)], rin_z.at[task, t - 1],
+            rz_out.at[task, t - 1], rz_in.at[task, t - 1], (r, (here + 1) * 4 + y * 2 + k),
+        )
+
+    def left_copy(task, c, part, here, t):
+        return remote(
+            p.at[c, at(part * rows + t * block, block)], lin.at[task, t],
+            lz_out.at[task, t], lz_in.at[task, t], (r, (here - 1) * 4 + y * 2 + k),
         )
 
     def add_to(c, part, low, high, *arrived):
@@ -128,76 +125,71 @@
             value += ref.astype(jnp.float32)
         p[c, where] = value.astype(jnp.bfloat16)
 
-    def from_left(task, low, high):
-        return rin_z[task, pl.ds((low - 1) * block, (high - low) * block)]
-
-    def from_right(task, low, high):
-        return lin[task, pl.ds(low * block, (high - low) * block)]
+    def pass_right(task, c, part, here, t):
+        right_copy(task, c, part, here - 1, t).wait_recv()
+        add_to(c, part, t, t + 1, rin_z[task, t - 1])
+        right_copy(task, c, part, here, t).start()
+
+    def pass_left(task, c, part, here, t):
+        left_copy(task, c, part, here + 1, t).wait_recv()
+        add_to(c, part, t, t + 1, lin[task, t])
+        left_copy(task, c, part, here, t).start()
 
     def line_start(task, c, part):
         @pl.when(z == 0)
         def _():
-            right_copy(task, c, part, 0).start()
+            for t in (3, 2, 1):
+                right_copy(task, c, part, 0, t).start()
 
         @pl.when(z == 3)
         def _():
-            left_copy(task, c, part, 3).start()
+            for t in (0, 1, 2):
+                left_copy(task, c, part, 3, t).start()
 
     def line_inward(task, c, part):
         @pl.when(z == 1)
         def _():
-            right_copy(task, c, part, 0).wait_recv()
-            add_to(c, part, 2, 4, from_left(task, 2, 4))
-            right_copy(task, c, part, 1).start()
+            for t in (3, 2):
+                pass_right(task, c, part, 1, t)
 
         @pl.when(z == 2)
         def _():
-            left_copy(task, c, part, 3).wait_recv()
-            add_to(c, part, 0, 2, from_right(task, 0, 2))
-            left_copy(task, c, part, 2).start()
+            for t in (0, 1):
+                pass_left(task, c, part, 2, t)
 
     def line_outward(task, c, part):
         @pl.when(z == 1)
         def _():
-            left_copy(task, c, part, 2).wait_recv()
-            add_to(c, part, 0, 1, from_right(task, 0, 1))
-            left_copy(task, c, part, 1).start()
+            pass_left(task, c, part, 1, 0)
 
         @pl.when(z == 2)
         def _():
-            right_copy(task, c, part, 1).wait_recv()
-            add_to(c, part, 3, 4, from_left(task, 3, 4))
-            right_copy(task, c, part, 2).start()
+            pass_right(task, c, part, 2, 3)
 
     def line_end(task, c, part):
-        @pl.when(z == 0)
-        def _():
-            left_copy(task, c, part, 1).wait_recv()
-            add_to(c, part, 0, 1, from_right(task, 0, 1))
-
-        @pl.when(z == 3)
-        def _():
-            right_copy(task, c, part, 2).wait_recv()
-            add_to(c, part, 3, 4, from_left(task, 3, 4))
-
-        for here in (1, 2):
+        for here in range(LAYERS_Z):
 
             @pl.when(z == here)
             def _(here=here):
-                add_to(
-                    c, part, here, here + 1,
-                    from_left(task, here, here + 1), from_right(task, here, here + 1),
-                )
+                arrived = []
+                if here > 0:
+                    right_copy(task, c, part, here - 1, here).wait_recv()
+                    arrived.append(rin_z[task, here - 1])
+                if here < LAYERS_Z - 1:
+                    left_copy(task, c, part, here + 1, here).wait_recv()
+                    arrived.append(lin[task, here])
+                add_to(c, part, here, here + 1, *arrived)
 
     def line_sent(task, c, part):
         for here in range(LAYERS_Z):
 
             @pl.when(z == here)
             def _(here=here):
-                if here < LAYERS_Z - 1:
-                    right_copy(task, c, part, here).wait_send()
-                if here > 0:
-                    left_copy(task, c, part, here).wait_send()
+                for t in range(LAYERS_Z):
+                    if t > here:
+                        right_copy(task, c, part, here, t).wait_send()
+                    if t < here:
+                        left_copy(task, c, part, here, t).wait_send()
 
     def core_copy(c):
         return remote(
@@ -223,9 +215,13 @@
     grads_in = pltpu.make_async_copy(grads, g, loads.at[0])
     grads_in.start()
 
-    @pl.loop(0, chunks)
+    @pl.loop(0, AHEAD)
     def _(c):
         acts_local(c).start()
+
+    @pl.loop(0, firsts)
+    def _(c):
+        acts_local(plains + c).start()
 
     others = [
         pltpu.make_async_copy(x, v, loads.at[1 + j])
@@ -233,9 +229,6 @@
             ((weight, wv), (mean, mv), (var, vv), (glob, gv), (outer, ov))
         )
     ]
-    for copy in others:
-        copy.start()
-
     barrier = pltpu.get_barrier_semaphore()
     for peer in (other_core, other_y, other_worker):
         pl.semaphore_signal(barrier, inc=1, device_id=peer, device_id_type=pl.DeviceIdType.MESH)
@@ -266,17 +259,9 @@
     gt_copy.start()
 
     acts_remote(0).start()
-
-    @pl.loop(0, firsts)
-    def _(j):
-        acts_remote(plains + j).start()
-        acts_remote(1 + j).start()
-
-    @pl.loop(1 + firsts, plains)
-    def _(c):
-        acts_remote(c).start()
-
-    weight_copy.start()
+    acts_remote(1).start()
+    acts_remote(plains).start()
+    acts_remote(2).start()
     gt_copy.wait_recv()
 
     time = jnp.full((1, cols), count[0].astype(jnp.float32))
@@ -357,6 +342,15 @@
             y_copy(c).start()
             product(c, y)
 
+        @pl.when(i + AHEAD < plains)
+        def _():
+            acts_local(i + AHEAD).start()
+            acts_remote(i + AHEAD).start()
+
+        @pl.when(i < firsts - 1)
+        def _():
+            acts_remote(plains + 1 + i).start()
+
         @first_at(1)
         def _(c):
             fetched(c)
@@ -364,59 +358,23 @@
             product(c, y)
             halves(line_start, c)
 
+        @pl.when(i == 1)
+        def _():
+            weight_copy.start()
+            for copy in others:
+                copy.start()
+
+        @first_at(plains)
+        def _(c):
+            late_y_copy(c).start()
+
         @plain_at(LAG_Y)
         def _(c):
             y_copy(c).wait_recv()
             add_to(c, y, 0, LAYERS_Z, yin[c])
             line_start(c, c, y)
 
-        @first_at(4)
-        def _(c):
-            halves(line_inward, c)
-
-        @plain_at(LAG_Z)
-        def _(c):
-            line_inward(c, c, y)
-
-        @first_at(6)
-        def _(c):
-            halves(line_outward, c)
-
-        @plain_at(LAG_Z + 1)
-        def _(c):
-            line_outward(c, c, y)
-
-        @first_at(8)
-        def _(c):
-            halves(line_end, c)
-            late_y_copy(c).start()
-
-        @plain_at(LAG_Z + 2)
-        def _(c):
-            line_end(c, c, y)
-            to_core(c)
-
-        @pl.when(i == LAG_Z + 3)
-        def _():
-            for copy in others:
-                copy.wait()
-            weight_copy.wait()
-
-        @plain_at(LAG_Z + 3)
-        def _(c):
-            adam(c)
-
-        @plain_at(LAG_Z + 4)
-        def _(c):
-            update(c)
-
-        @plain_at(LAG_DONE)
-        def _(c):
-            y_copy(c).wait_send()
-            line_sent(c, c, y)
-            done(c)
-
-        @first_at(12)
+        @first_at(plains + LAG_Y + 1)
         def _(c):
             late_y_copy(c).wait_recv()
             where = at(y * rows + z * block, block)
@@ -425,21 +383,77 @@
             ).astype(jnp.bfloat16)
             to_core(c)
 
-        @first_at(13)
+        @first_at(plains + LAG_Y + 2)
         def _(c):
             adam(c)
 
-        @first_at(14)
+        @first_at(plains + LAG_Y + 3)
         def _(c):
             update(c)
 
-        @first_at(15)
+        @first_at(plains + LAG_Y + 4)
         def _(c):
             late_y_copy(c).wait_send()
             halves(line_sent, c)
             done(c)
 
+        @first_at(4)
+        def _(c):
+            halves(line_inward, c)
+
+        @plain_at(LAG_Z)
+        def _(c):
+            line_inward(c, c, y)
+
+        @first_at(6)
+        def _(c):
+            halves(line_outward, c)
+
+        @plain_at(LAG_Z + 1)
+        def _(c):
+            line_outward(c, c, y)
+
+        @first_at(8)
+        def _(c):
+            halves(line_end, c)
+
+        @plain_at(LAG_Z + 2)
+        def _(c):
+            line_end(c, c, y)
+            to_core(c)
+
+        @pl.when(i == LAG_Z + 3)
+        def _():
+            for copy in others:
+                copy.wait()
+            weight_copy.wait()
+
+        @plain_at(LAG_Z + 3)
+        def _(c):
+            adam(c)
+
+        @plain_at(LAG_Z + 4)
+        def _(c):
+            update(c)
+
+        @plain_at(LAG_DONE)
+        def _(c):
+            y_copy(c).wait_send()
+            line_sent(c, c, y)
+            done(c)
+
     gt_copy.wait_send()
+
+
+def place(a, b, c, to_a, to_b, to_c, sems):
+    copies = [
+        pltpu.make_async_copy(x, to, sems.at[j])
+        for j, (x, to) in enumerate(((a, to_a), (b, to_b), (c, to_c)))
+    ]
+    for copy in copies:
+        copy.start()
+    for copy in copies:
+        copy.wait()
 
 
 def fused(
@@ -456,13 +470,14 @@
     vmem, dma = pltpu.VMEM, pltpu.SemaphoreType.DMA
     n = CHUNKS
     tasks = n + ZFIRST * (ROWS_Y - 1)
-    return pl.pallas_call(
+    shapes = (
+        jax.ShapeDtypeStruct((units, width), b16),
+        jax.ShapeDtypeStruct((units, half), f32),
+        jax.ShapeDtypeStruct((units, half), f32),
+    )
+    results = pl.pallas_call(
         functools.partial(kernel, factor),
-        out_shape=(
-            jax.ShapeDtypeStruct((units, width), b16),
-            jax.ShapeDtypeStruct((units, half), f32),
-            jax.ShapeDtypeStruct((units, half), f32),
-        ),
+        out_shape=shapes,
         in_specs=[pl.BlockSpec(memory_space=pl.ANY)] * 7
         + [pl.BlockSpec(memory_space=pltpu.SMEM)],
         out_specs=[pl.BlockSpec(memory_space=pl.ANY)] * 3,
@@ -473,8 +488,8 @@
             vmem((n, features, cols), b16),
             vmem((n - ZFIRST, rows, cols), b16),
             vmem((ZFIRST, CORES * units, cols), b16),
-            vmem((tasks, (LAYERS_Z - 1) * CORES * units, cols), b16),
-            vmem((tasks, (LAYERS_Z - 1) * CORES * units, cols), b16),
+            vmem((tasks, LAYERS_Z - 1, CORES * units, cols), b16),
+            vmem((tasks, LAYERS_Z - 1, CORES * units, cols), b16),
             vmem((n, CORES, units, cols), b16),
             vmem((n, units, cols), b16),
             vmem((n, units, cols), b16),
@@ -489,7 +504,7 @@
             vmem((units, half), f32),
             vmem((units, half), b16),
             dma((n,)), dma((n,)), dma((n,)), dma, dma,
-            dma((n,)), dma((n,)), *[dma((tasks,))] * 4,
+            dma((n,)), dma((n,)), *[dma((tasks, LAYERS_Z - 1))] * 4,
             dma((n,)), dma((n,)), dma((n,)), dma((n,)),
             dma((n,)), dma((n,)), dma, dma, dma((6,)), dma((3, n)),
         ],
@@ -503,6 +518,14 @@
         acts, out_grads, local_weight[0], adam_mean[0], adam_var[0],
         global_weight, outer_momentum, step_count,
     )
+    return pl.pallas_call(
+        place,
+        out_shape=shapes,
+        in_specs=[pl.BlockSpec(memory_space=pl.ANY)] * 3,
+        out_specs=[pl.BlockSpec(memory_space=pl.ANY)] * 3,
+        scratch_shapes=[dma((3,))],
+        compiler_params=pltpu.CompilerParams(vmem_limit_bytes=56 * 2**20),
+    )(*results)
 
 
 def solution(mesh):

time: 123 us -> 211 us (1.72)
  Pallas kernels: 117 us -> 210 us
  local copies, waits for them, and re-layouts: 4.36 us -> 0 us
    pallas_call x1 -> x2, Pallas kernels: 117 us -> 210 us  [the longest x1 114 us: fused(): pl.pallas_call(functools.partial(kernel, factor), out_shape=shapes, in_sp...]
    unnamed x7 -> x0, local copies, waits for them, and re-layouts: 4.36 us -> none
where the time goes in v4:
time: 211 us
  Pallas kernels  210 us (100%)
    pallas_call x1, Pallas kernels, fused(): pl.pallas_call(functools.partial(kernel, factor), out_shape=shapes, in_sp...  114 us
    pallas_call x1, Pallas kernels, fused(): pl.pallas_call(place, out_shape=shapes, in_specs=[pl.BlockSpec(memory_spa...  96.4 us

profile of v4, /device:TPU:0, one launch (start us, length us, event | category | flops | bytes accessed | tf_op | source)
XLA Modules:
  0.0 211.2 jit_solution(4613659035349452259)
XLA Ops:
  1.3 113.5 %shard_map.103 = (bf16[64,8192]{1,0:T(8,128)(2,1)}, f32[64,4096]{1,0:T(8,128)}, f32[64,4096]{1,0:T(8,128)}) custom-call(bf16[512,8192]{1,0:T(8,128)(2,1)} %acts.1, bf16[512,1024]{1,0:T(8,128)(2,1)} %grads.1, bf16[64,8192]{1,0:T(8,128)(2,1)} %bitcast.5, f32[64,8192]{1,0:T(8,128)} %bitcast.3, f32[64,8192]{1,0:T(8,128)} %bitcast.4, f32[64,4096]{1,0:T(8,128)} %glob.1, ...), custom_call_target="tpu_custom_call" | custom-call | flops 8589934592 | bytes 25165824 | tf_op jit(solution)/shard_map/pallas_call | solution.py:478
  114.8 96.4 %shard_map.104 = (bf16[64,8192]{1,0:T(8,128)(2,1)}, f32[64,4096]{1,0:T(8,128)}, f32[64,4096]{1,0:T(8,128)}) custom-call(bf16[64,8192]{1,0:T(8,128)(2,1)} %get-tuple-element.6.a, f32[64,4096]{1,0:T(8,128)} %get-tuple-element.7.b, f32[64,4096]{1,0:T(8,128)} %get-tuple-element.8.c), custom_call_target="tpu_custom_call" | custom-call | tf_op jit(solution)/shard_map/pallas_call | solution.py:521

commit v5 on v4

--- a/solution.py
+++ b/solution.py
@@ -54,8 +54,8 @@
 def kernel(
     factor, acts, grads, weight, mean, var, glob, outer, count,
     synced, new_glob, new_mom,
-    a, g, gt, p, yin, ybin, lin, rin_z, gbuf, rout, rin, acc, ng, nm, sy, wv, mv, vv, gv, ov, wo,
-    a_loc, a_out, a_in, gt_out, gt_in, y_out, y_in, rz_out, rz_in, lz_out, lz_in, c_out, c_in, r_out, r_in,
+    a, stage, g, gt, p, yin, ybin, lin, rin_z, gbuf, rout, rin, acc, ng, nm, sy, wv, mv, vv, gv, ov, wo,
+    a_loc, st_loc, a_out, a_in, gt_out, gt_in, y_out, y_in, rz_out, rz_in, lz_out, lz_in, c_out, c_in, r_out, r_in,
     s_out, s_in, w_out, w_in, loads, stores,
 ):
     r = lax.axis_index("worker")
@@ -89,11 +89,23 @@
             acts.at[:, at(k * half + c * cols)], a.at[c, pl.ds(0, tokens)], a_loc.at[c]
         )
 
+    def acts_staged(c):
+        return pltpu.make_async_copy(
+            acts.at[:, at((1 - k) * half + c * cols)], stage.at[c], st_loc.at[c]
+        )
+
     def acts_remote(c):
         return remote(
-            acts.at[:, at((1 - k) * half + c * cols)], a.at[c, pl.ds(tokens, tokens)],
-            a_out.at[c], a_in.at[c], other_core,
-        )
+            stage.at[c], a.at[c, pl.ds(tokens, tokens)], a_out.at[c], a_in.at[c], other_core
+        )
+
+    def load_acts(c):
+        acts_staged(c).start()
+        acts_local(c).start()
+
+    def send_acts(c):
+        acts_staged(c).wait()
+        acts_remote(c).start()
 
     def y_copy(c):
         return remote(
@@ -215,13 +227,9 @@
     grads_in = pltpu.make_async_copy(grads, g, loads.at[0])
     grads_in.start()
 
-    @pl.loop(0, AHEAD)
-    def _(c):
-        acts_local(c).start()
-
-    @pl.loop(0, firsts)
-    def _(c):
-        acts_local(plains + c).start()
+    load_acts(0)
+    load_acts(1)
+    load_acts(plains)
 
     others = [
         pltpu.make_async_copy(x, v, loads.at[1 + j])
@@ -253,15 +261,24 @@
         gt.at[:, pl.ds(0, tokens)], gt.at[:, pl.ds(tokens, tokens)], gt_out, gt_in, other_core
     )
     weight_copy = remote(
-        weight.at[:, at((1 - r) * half, half)], wo, w_out, w_in, other_worker
+        wv.at[:, at((1 - r) * half, half)], wo, w_out, w_in, other_worker
     )
     pl.semaphore_wait(barrier, 4 + lax.rem(lax.div(z + 1, 2), 2))
     gt_copy.start()
 
-    acts_remote(0).start()
-    acts_remote(1).start()
-    acts_remote(plains).start()
-    acts_remote(2).start()
+    send_acts(0)
+    send_acts(1)
+    send_acts(plains)
+
+    @pl.loop(2, plains)
+    def _(c):
+        load_acts(c)
+
+    @pl.loop(plains + 1, chunks)
+    def _(c):
+        load_acts(c)
+
+    send_acts(2)
     gt_copy.wait_recv()
 
     time = jnp.full((1, cols), count[0].astype(jnp.float32))
@@ -344,12 +361,11 @@
 
         @pl.when(i + AHEAD < plains)
         def _():
-            acts_local(i + AHEAD).start()
-            acts_remote(i + AHEAD).start()
+            send_acts(i + AHEAD)
 
         @pl.when(i < firsts - 1)
         def _():
-            acts_remote(plains + 1 + i).start()
+            send_acts(plains + 1 + i)
 
         @first_at(1)
         def _(c):
@@ -360,9 +376,14 @@
 
         @pl.when(i == 1)
         def _():
-            weight_copy.start()
             for copy in others:
                 copy.start()
+
+        @pl.when(i == 3)
+        def _():
+            for copy in others:
+                copy.wait()
+            weight_copy.start()
 
         @first_at(plains)
         def _(c):
@@ -424,8 +445,6 @@
 
         @pl.when(i == LAG_Z + 3)
         def _():
-            for copy in others:
-                copy.wait()
             weight_copy.wait()
 
         @plain_at(LAG_Z + 3)
@@ -445,14 +464,23 @@
     gt_copy.wait_send()
 
 
-def place(a, b, c, to_a, to_b, to_c, sems):
-    copies = [
-        pltpu.make_async_copy(x, to, sems.at[j])
-        for j, (x, to) in enumerate(((a, to_a), (b, to_b), (c, to_c)))
-    ]
-    for copy in copies:
+def place(a, b, c, to_a, to_b, to_c, held_a, held_b, held_c, sems, out_sems):
+    pieces = 2
+    loads, stores = [], []
+    for p in range(pieces):
+        for j, (x, held, to) in enumerate(
+            ((a, held_a, to_a), (b, held_b, to_b), (c, held_c, to_c))
+        ):
+            size = x.shape[0] // pieces
+            rows = pl.ds(p * size, size)
+            loads.append(pltpu.make_async_copy(x.at[rows], held.at[rows], sems.at[p, j]))
+            stores.append(pltpu.make_async_copy(held.at[rows], to.at[rows], out_sems.at[p, j]))
+    for copy in loads:
         copy.start()
-    for copy in copies:
+    for load, store in zip(loads, stores):
+        load.wait()
+        store.start()
+    for copy in stores:
         copy.wait()
 
 
@@ -483,6 +511,7 @@
         out_specs=[pl.BlockSpec(memory_space=pl.ANY)] * 3,
         scratch_shapes=[
             vmem((n, CORES * tokens, cols), b16),
+            vmem((n, tokens, cols), b16),
             vmem((tokens, features), b16),
             vmem((features, CORES * tokens), b16),
             vmem((n, features, cols), b16),
@@ -503,7 +532,7 @@
             vmem((units, half), f32),
             vmem((units, half), f32),
             vmem((units, half), b16),
-            dma((n,)), dma((n,)), dma((n,)), dma, dma,
+            dma((n,)), dma((n,)), dma((n,)), dma((n,)), dma, dma,
             dma((n,)), dma((n,)), *[dma((tasks, LAYERS_Z - 1))] * 4,
             dma((n,)), dma((n,)), dma((n,)), dma((n,)),
             dma((n,)), dma((n,)), dma, dma, dma((6,)), dma((3, n)),
@@ -523,7 +552,7 @@
         out_shape=shapes,
         in_specs=[pl.BlockSpec(memory_space=pl.ANY)] * 3,
         out_specs=[pl.BlockSpec(memory_space=pl.ANY)] * 3,
-        scratch_shapes=[dma((3,))],
+        scratch_shapes=[vmem(x.shape, x.dtype) for x in shapes] + [dma((2, 3)), dma((2, 3))],
         compiler_params=pltpu.CompilerParams(vmem_limit_bytes=56 * 2**20),
     )(*results)
 

time: 211 us -> 117 us (0.55)
  Pallas kernels: 210 us -> 116 us
    pallas_call x1, Pallas kernels: 96.4 us -> 2.8 us  [fused(): pl.pallas_call(place, out_shape=shapes, in_specs=[pl.BlockSpec(memory_spa...]
where the time goes in v5:
time: 117 us
  Pallas kernels  116 us (99%)
  between operations  1.29 us (1%)
    pallas_call x1, Pallas kernels, fused(): pl.pallas_call(functools.partial(kernel, factor), out_shape=shapes, in_sp...  113 us
    pallas_call x1, Pallas kernels, fused(): pl.pallas_call(place, out_shape=shapes, in_specs=[pl.BlockSpec(memory_spa...  2.8 us

profile of v5, /device:TPU:0, one launch (start us, length us, event | category | flops | bytes accessed | tf_op | source)
XLA Modules:
  0.0 117.0 jit_solution(983061716700972868)
XLA Ops:
  1.3 112.9 %shard_map.103 = (bf16[64,8192]{1,0:T(8,128)(2,1)}, f32[64,4096]{1,0:T(8,128)}, f32[64,4096]{1,0:T(8,128)}) custom-call(bf16[512,8192]{1,0:T(8,128)(2,1)} %acts.1, bf16[512,1024]{1,0:T(8,128)(2,1)} %grads.1, bf16[64,8192]{1,0:T(8,128)(2,1)} %bitcast.5, f32[64,8192]{1,0:T(8,128)} %bitcast.3, f32[64,8192]{1,0:T(8,128)} %bitcast.4, f32[64,4096]{1,0:T(8,128)} %glob.1, ...), custom_call_target="tpu_custom_call" | custom-call | flops 8589934592 | bytes 25165824 | tf_op jit(solution)/shard_map/pallas_call | solution.py:506
  114.2 2.8 %shard_map.104 = (bf16[64,8192]{1,0:T(8,128)(2,1)}, f32[64,4096]{1,0:T(8,128)}, f32[64,4096]{1,0:T(8,128)}) custom-call(bf16[64,8192]{1,0:T(8,128)(2,1)} %get-tuple-element.6.a, f32[64,4096]{1,0:T(8,128)} %get-tuple-element.7.b, f32[64,4096]{1,0:T(8,128)} %get-tuple-element.8.c), custom_call_target="tpu_custom_call" | custom-call | tf_op jit(solution)/shard_map/pallas_call | solution.py:550

commit v6 on v5

--- a/solution.py
+++ b/solution.py
@@ -257,18 +257,23 @@
     for j in range(g.shape[1] // block):
         place = (j % ROWS_Y) * LAYERS_Z + j // ROWS_Y
         gt[place * block : (place + 1) * block, 0:tokens] = g[:, j * block : (j + 1) * block].T
-    gt_copy = remote(
-        gt.at[:, pl.ds(0, tokens)], gt.at[:, pl.ds(tokens, tokens)], gt_out, gt_in, other_core
-    )
+    def gt_copy(side):
+        where = at(side * rows, rows)
+        return remote(
+            gt.at[where, pl.ds(0, tokens)], gt.at[where, pl.ds(tokens, tokens)],
+            gt_out.at[side], gt_in.at[side], other_core,
+        )
+
     weight_copy = remote(
         wv.at[:, at((1 - r) * half, half)], wo, w_out, w_in, other_worker
     )
     pl.semaphore_wait(barrier, 4 + lax.rem(lax.div(z + 1, 2), 2))
-    gt_copy.start()
+    gt_copy(1 - y).start()
 
     send_acts(0)
+    gt_copy(y).start()
+    send_acts(plains)
     send_acts(1)
-    send_acts(plains)
 
     @pl.loop(2, plains)
     def _(c):
@@ -279,7 +284,7 @@
         load_acts(c)
 
     send_acts(2)
-    gt_copy.wait_recv()
+    gt_copy(1 - y).wait_recv()
 
     time = jnp.full((1, cols), count[0].astype(jnp.float32))
     first = 1.0 / (1.0 - jnp.exp(time * math.log(0.9)))
@@ -357,6 +362,20 @@
             fetched(c)
             product(c, 1 - y)
             y_copy(c).start()
+
+        @pl.when(i == 0)
+        def _():
+            gt_copy(y).wait_recv()
+
+        @first_at(0)
+        def _(c):
+            fetched(c)
+            for h, part in enumerate((1 - y, y)):
+                product(c, part)
+                line_start(plains + (c - plains) * ROWS_Y + h, c, part)
+
+        @plain_at(0)
+        def _(c):
             product(c, y)
 
         @pl.when(i + AHEAD < plains)
@@ -366,13 +385,6 @@
         @pl.when(i < firsts - 1)
         def _():
             send_acts(plains + 1 + i)
-
-        @first_at(1)
-        def _(c):
-            fetched(c)
-            product(c, 1 - y)
-            product(c, y)
-            halves(line_start, c)
 
         @pl.when(i == 1)
         def _():
@@ -461,7 +473,8 @@
             line_sent(c, c, y)
             done(c)
 
-    gt_copy.wait_send()
+    gt_copy(0).wait_send()
+    gt_copy(1).wait_send()
 
 
 def place(a, b, c, to_a, to_b, to_c, held_a, held_b, held_c, sems, out_sems):
@@ -532,7 +545,7 @@
             vmem((units, half), f32),
             vmem((units, half), f32),
             vmem((units, half), b16),
-            dma((n,)), dma((n,)), dma((n,)), dma((n,)), dma, dma,
+            dma((n,)), dma((n,)), dma((n,)), dma((n,)), dma((2,)), dma((2,)),
             dma((n,)), dma((n,)), *[dma((tasks, LAYERS_Z - 1))] * 4,
             dma((n,)), dma((n,)), dma((n,)), dma((n,)),
             dma((n,)), dma((n,)), dma, dma, dma((6,)), dma((3, n)),

time: 117 us -> 116 us (level)
  Pallas kernels: 116 us -> 114 us
    pallas_call x1, Pallas kernels: 113 us -> 111 us  [fused(): pl.pallas_call(functools.partial(kernel, factor), out_shape=shapes, in_sp...]
where the time goes in v6:
time: 116 us
  Pallas kernels  114 us (98%)
  between operations  1.29 us (1%)
    pallas_call x1, Pallas kernels, fused(): pl.pallas_call(functools.partial(kernel, factor), out_shape=shapes, in_sp...  111 us
    pallas_call x1, Pallas kernels, fused(): pl.pallas_call(place, out_shape=shapes, in_specs=[pl.BlockSpec(memory_spa...  2.8 us

profile of v6, /device:TPU:0, one launch (start us, length us, event | category | flops | bytes accessed | tf_op | source)
XLA Modules:
  0.0 115.6 jit_solution(10058601983255094978)
XLA Ops:
  1.3 111.5 %shard_map.103 = (bf16[64,8192]{1,0:T(8,128)(2,1)}, f32[64,4096]{1,0:T(8,128)}, f32[64,4096]{1,0:T(8,128)}) custom-call(bf16[512,8192]{1,0:T(8,128)(2,1)} %acts.1, bf16[512,1024]{1,0:T(8,128)(2,1)} %grads.1, bf16[64,8192]{1,0:T(8,128)(2,1)} %bitcast.5, f32[64,8192]{1,0:T(8,128)} %bitcast.3, f32[64,8192]{1,0:T(8,128)} %bitcast.4, f32[64,4096]{1,0:T(8,128)} %glob.1, ...), custom_call_target="tpu_custom_call" | custom-call | flops 8589934592 | bytes 25165824 | tf_op jit(solution)/shard_map/pallas_call | solution.py:519
  112.8 2.8 %shard_map.104 = (bf16[64,8192]{1,0:T(8,128)(2,1)}, f32[64,4096]{1,0:T(8,128)}, f32[64,4096]{1,0:T(8,128)}) custom-call(bf16[64,8192]{1,0:T(8,128)(2,1)} %get-tuple-element.6.a, f32[64,4096]{1,0:T(8,128)} %get-tuple-element.7.b, f32[64,4096]{1,0:T(8,128)} %get-tuple-element.8.c), custom_call_target="tpu_custom_call" | custom-call | tf_op jit(solution)/shard_map/pallas_call | solution.py:563

commit v7 on v6

--- a/solution.py
+++ b/solution.py
@@ -14,9 +14,9 @@
 CHUNKS = 16
 ZFIRST = 3
 AHEAD = 3
-LAG_Y = 2
-LAG_Z = 5
-LAG_DONE = 10
+LAG_Y = 3
+LAG_Z = 6
+LAG_DONE = 11
 
 
 def inner_step(weight, mean, var, grad, count):

time: 116 us -> 116 us (level)
  no operation moved by 1% of the time
where the time goes in v7:
time: 116 us
  Pallas kernels  114 us (98%)
  between operations  1.29 us (1%)
    pallas_call x1, Pallas kernels, fused(): pl.pallas_call(functools.partial(kernel, factor), out_shape=shapes, in_sp...  111 us
    pallas_call x1, Pallas kernels, fused(): pl.pallas_call(place, out_shape=shapes, in_specs=[pl.BlockSpec(memory_spa...  2.8 us

profile of v7, /device:TPU:0, one launch (start us, length us, event | category | flops | bytes accessed | tf_op | source)
XLA Modules:
  0.0 115.6 jit_solution(16053174798562395048)
XLA Ops:
  1.3 111.5 %shard_map.103 = (bf16[64,8192]{1,0:T(8,128)(2,1)}, f32[64,4096]{1,0:T(8,128)}, f32[64,4096]{1,0:T(8,128)}) custom-call(bf16[512,8192]{1,0:T(8,128)(2,1)} %acts.1, bf16[512,1024]{1,0:T(8,128)(2,1)} %grads.1, bf16[64,8192]{1,0:T(8,128)(2,1)} %bitcast.5, f32[64,8192]{1,0:T(8,128)} %bitcast.3, f32[64,8192]{1,0:T(8,128)} %bitcast.4, f32[64,4096]{1,0:T(8,128)} %glob.1, ...), custom_call_target="tpu_custom_call" | custom-call | flops 8589934592 | bytes 25165824 | tf_op jit(solution)/shard_map/pallas_call | solution.py:519
  112.8 2.8 %shard_map.104 = (bf16[64,8192]{1,0:T(8,128)(2,1)}, f32[64,4096]{1,0:T(8,128)}, f32[64,4096]{1,0:T(8,128)}) custom-call(bf16[64,8192]{1,0:T(8,128)(2,1)} %get-tuple-element.6.a, f32[64,4096]{1,0:T(8,128)} %get-tuple-element.7.b, f32[64,4096]{1,0:T(8,128)} %get-tuple-element.8.c), custom_call_target="tpu_custom_call" | custom-call | tf_op jit(solution)/shard_map/pallas_call | solution.py:563

commit v8 on v7

--- a/solution.py
+++ b/solution.py
@@ -12,7 +12,7 @@
 ROWS_Y = 2
 LAYERS_Z = 4
 CHUNKS = 16
-ZFIRST = 3
+ZFIRST = 2
 AHEAD = 3
 LAG_Y = 3
 LAG_Z = 6

time: 116 us -> 121 us (1.043)
  Pallas kernels: 114 us -> 119 us
    pallas_call x1, Pallas kernels: 111 us -> 116 us  [fused(): pl.pallas_call(functools.partial(kernel, factor), out_shape=shapes, in_sp...]
where the time goes in v8:
time: 121 us
  Pallas kernels  119 us (98%)
  between operations  1.29 us (1%)
    pallas_call x1, Pallas kernels, fused(): pl.pallas_call(functools.partial(kernel, factor), out_shape=shapes, in_sp...  116 us
    pallas_call x1, Pallas kernels, fused(): pl.pallas_call(place, out_shape=shapes, in_specs=[pl.BlockSpec(memory_spa...  2.8 us

profile of v8, /device:TPU:0, one launch (start us, length us, event | category | flops | bytes accessed | tf_op | source)
XLA Modules:
  0.0 120.6 jit_solution(5806456613062044493)
XLA Ops:
  1.3 116.5 %shard_map.103 = (bf16[64,8192]{1,0:T(8,128)(2,1)}, f32[64,4096]{1,0:T(8,128)}, f32[64,4096]{1,0:T(8,128)}) custom-call(bf16[512,8192]{1,0:T(8,128)(2,1)} %acts.1, bf16[512,1024]{1,0:T(8,128)(2,1)} %grads.1, bf16[64,8192]{1,0:T(8,128)(2,1)} %bitcast.5, f32[64,8192]{1,0:T(8,128)} %bitcast.3, f32[64,8192]{1,0:T(8,128)} %bitcast.4, f32[64,4096]{1,0:T(8,128)} %glob.1, ...), custom_call_target="tpu_custom_call" | custom-call | flops 8589934592 | bytes 25165824 | tf_op jit(solution)/shard_map/pallas_call | solution.py:519
  117.8 2.8 %shard_map.104 = (bf16[64,8192]{1,0:T(8,128)(2,1)}, f32[64,4096]{1,0:T(8,128)}, f32[64,4096]{1,0:T(8,128)}) custom-call(bf16[64,8192]{1,0:T(8,128)(2,1)} %get-tuple-element.6.a, f32[64,4096]{1,0:T(8,128)} %get-tuple-element.7.b, f32[64,4096]{1,0:T(8,128)} %get-tuple-element.8.c), custom_call_target="tpu_custom_call" | custom-call | tf_op jit(solution)/shard_map/pallas_call | solution.py:563
